TPU v7x, 32 devices: a whole 2x2x4 slice. The times are simulated.
32 devices in a mesh: groups: 2 (over y), date: 4 (over z), pix: 2 (over x), chan: 2 (over core).
Axes of the slice: x: 2, y: 2, z: 4, core: 2. Of those that a mesh axis runs over, the one named last changes fastest.
Arguments:
- frames: bfloat16 [128, 4, 64, 128], P(('groups', 'date'), 'pix'), parts along dimension 0, may hold values from -6 to 6
- spatial_weight: bfloat16 [3, 3, 64, 64], P(None, None, None, 'chan'), may hold values from -0.25 to 0.25
- spatial_bias: float32 [64], P('chan'), may hold values from -3 to 3
- temporal_weight: bfloat16 [64, 64, 16], P('date', 'chan'), may hold values from -0.1875 to 0.1875
- temporal_bias: float32 [16], replicated, may hold values from -4 to 4
- head_weight: float32 [16], replicated, may hold values from -3 to 3
- labels: int32 [8, 128], P(('groups', 'pix'), ('date', 'chan')), parts along dimension 0, may hold values 0 or 1
Outputs:
- logits: float32 [8, 128], P(('groups', 'pix'), ('date', 'chan')), parts along dimension 0
- grad_spatial: float32 [6, 3, 64, 64], P('groups', None, None, 'chan'), parts along dimension 0
- grad_temporal: float32 [64, 64, 32], P('date', 'chan', 'groups'), parts along dimension 2
There are 2 independent parts, one for each index of `groups`. A program takes and returns all parts, laid end to end along the dimension named above; an argument that names none is the same for every part. Nothing has to cross between parts.
All inputs are finite; a program needn't handle non-finite values. No bound on the sum of `labels` on one device may be relied on, other than what follows from the above.
Results may differ from a plain program's by a relative error of at most 0.024.
Values may be sent and summed in bfloat16 or wider, within the bound.
A program may use at most 64 MiB of HBM per device.

v0:
```python
import jax
import jax.numpy as jnp
from jax import lax
from jax.sharding import PartitionSpec as P


def with_halo(block, sides, width):
    for axis, dim in sides:
        count = lax.axis_size(axis)
        forward = [(i, i + 1) for i in range(count - 1)]
        backward = [(target, source) for source, target in forward]
        low = lax.ppermute(
            lax.slice_in_dim(block, block.shape[dim] - width, None, axis=dim), axis, forward
        )
        high = lax.ppermute(lax.slice_in_dim(block, 0, width, axis=dim), axis, backward)
        block = jnp.concatenate([low, block, high], axis=dim)
    return block


def shards(
    frames, spatial_weight, spatial_bias, temporal_weight, temporal_bias, head_weight, labels
):
    dates_here, rows, channels, columns = frames.shape
    padded = with_halo(frames, (("pix", 1),), 1)
    padded = jnp.pad(padded, ((0, 0), (0, 0), (0, 0), (1, 1)))
    preact = spatial_bias[None, None, :, None]
    for row_off in range(3):
        for col_off in range(3):
            window = padded[:, row_off : row_off + rows, :, col_off : col_off + columns]
            preact = preact + jnp.einsum(
                "ticj,co->tioj",
                window,
                spatial_weight[row_off, col_off],
                preferred_element_type=jnp.float32,
            )
    sigmoid_pre = jax.nn.sigmoid(preact)
    hidden = (preact * sigmoid_pre).astype(jnp.bfloat16)
    partial_feat = jnp.einsum(
        "tioj,tof->fij", hidden, temporal_weight, preferred_element_type=jnp.float32
    )
    feature = (
        lax.psum_scatter(partial_feat, ("date", "chan"), scatter_dimension=2, tiled=True)
        + temporal_bias[:, None, None]
    )
    sigmoid_feat = jax.nn.sigmoid(feature)
    logits = jnp.einsum("fij,f->ij", feature * sigmoid_feat, head_weight)
    dlogit = jax.nn.sigmoid(logits) - labels.astype(jnp.float32)
    feature_grad = (
        dlogit[None]
        * head_weight[:, None, None]
        * sigmoid_feat
        * (1.0 + feature * (1.0 - sigmoid_feat))
    ).astype(jnp.bfloat16)
    full_grad = lax.all_gather(feature_grad, ("date", "chan"), axis=2, tiled=True)
    temporal_part = jnp.einsum(
        "tioj,fij->tof", hidden, full_grad, preferred_element_type=jnp.float32
    )
    hidden_grad = jnp.einsum(
        "fij,tof->tioj", full_grad, temporal_weight, preferred_element_type=jnp.float32
    )
    preact_grad = (hidden_grad * sigmoid_pre * (1.0 + preact * (1.0 - sigmoid_pre))).astype(
        jnp.bfloat16
    )
    rows_out = []
    for row_off in range(3):
        cols_out = []
        for col_off in range(3):
            window = padded[:, row_off : row_off + rows, :, col_off : col_off + columns]
            cols_out.append(
                jnp.einsum("ticj,tioj->co", window, preact_grad, preferred_element_type=jnp.float32)
            )
        rows_out.append(jnp.stack(cols_out))
    spatial_part = jnp.stack(rows_out)
    grad_temporal = lax.psum(temporal_part, "pix")
    grad_spatial = lax.psum(spatial_part, ("date", "pix"))
    return (logits, grad_spatial, grad_temporal)


def solution(mesh):
    placed = (
        P(("groups", "date"), "pix", None, None),
        P(None, None, None, "chan"),
        P("chan"),
        P("date", "chan", None),
        P(),
        P(),
        P(("groups", "pix"), ("date", "chan")),
    )
    return jax.shard_map(
        shards,
        mesh=mesh,
        in_specs=placed,
        out_specs=(
            P(("groups", "pix"), ("date", "chan")),
            P("groups", None, None, "chan"),
            P("date", "chan", "groups"),
        ),
        check_vma=False,
    )
```

profile of v0, /device:TPU:0, one launch (start us, length us, event | category | flops | bytes accessed | tf_op | source)
XLA Modules:
  0.0 157.4 jit_solution(17748076628413484052)
XLA Ops:
  7.2 0.0 reduce-scatter.4.cloned.1.call-start
  7.2 1.1 fusion.79
  8.4 4.9 %collective-permute-start = (bf16[16,1,64,128]{3,2,1,0:T(8,128)(2,1)S(1)}, bf16[16,1,64,128]{3,2,1,0:T(8,128)(2,1)S(1)}, u32[]{:S(2)}, u32[]{:S(2)}) collective-permute-start(bf16[16,1,64,128]{3,2,1,0:T(8,128)(2,1)S(1)} %get-tuple-element.11), channel_id=1, source_target_pairs={{0,2},{1,3},{4,6},{5,7},{8,10},{9,11},{12,14},{13,15},{16,18},{17,... | collective-permute-start | bytes 786440 | tf_op jit(solution)/shard_map/ppermute | solution.py:12
  13.3 1.4 collective-permute-start.1
  14.7 1.3 fusion.47
  16.0 2.8 %collective-permute-done = bf16[16,1,64,128]{3,2,1,0:T(8,128)(2,1)S(1)} collective-permute-done((bf16[16,1,64,128]{3,2,1,0:T(8,128)(2,1)S(1)}, bf16[16,1,64,128]{3,2,1,0:T(8,128)(2,1)S(1)}, u32[]{:S(2)}, u32[]{:S(2)}) %collective-permute-start) | collective-permute-done | bytes 262176 | tf_op jit(solution)/shard_map/ppermute | solution.py:12
  18.8 4.3 %collective-permute-done.1 = bf16[16,1,64,128]{3,2,1,0:T(8,128)(2,1)S(1)} collective-permute-done((bf16[16,1,64,128]{3,2,1,0:T(8,128)(2,1)S(1)}, bf16[16,1,64,128]{3,2,1,0:T(8,128)(2,1)S(1)}, u32[]{:S(2)}, u32[]{:S(2)}) %collective-permute-start.1) | collective-permute-done | bytes 262176 | tf_op jit(solution)/shard_map/ppermute | solution.py:15
  23.0 1.1 fusion.5
  24.2 0.4 fusion.40
  24.5 0.4 fusion.51
  24.9 0.2 fusion.49
  25.1 0.2 fusion.44
  25.3 0.1 pad_maximum_fusion.1
  25.4 0.2 fusion.53
  25.6 0.2 fusion.42
  25.9 0.1 copy-done.15
  26.0 0.2 fusion.15
  26.2 1.2 multiply_convert_fusion
  27.4 0.2 convolution_bitcast_fusion.2
  27.6 0.8 copy.76
  28.4 1.7 %reshape.35 = f32[128,32]{1,0:T(8,128)} reshape(f32[128,2,16]{2,1,0:T(2,128)} %bitcast.179) | data formatting | bytes 32768
  30.1 0.0 all-reduce.3.cloned.1.call-start
  30.2 2.2 %fusion.78 = (bf16[16,2,64,128]{3,2,1,0:T(8,128)(2,1)}, bf16[16,2,64,128]{3,2,1,0:T(8,128)(2,1)}, bf16[16,2,64,128]{3,2,1,0:T(8,128)(2,1)}, bf16[16,2,64,128]{3,...) fusion(bf16[16,4,64,130]{3,2,1,0:T(8,128)(2,1)S(1)} %fusion.5), kind=kLoop, calls=%fused_computation.104 | loop fusion | bytes 6291456 | tf_op jit(solution)/shard_map/slice | solution.py:29
  32.4 28.2 %reduce-scatter.4.cloned.1.call-done = f32[16,32]{1,0:T(8,128)} async-done(((f32[128,32]{1,0:T(8,128)}), f32[16,32]{1,0:T(8,128)}) %reduce-scatter.4.cloned.1.call-update) | async-done | bytes 2064
  60.6 0.8 reshape.36
  61.4 0.1 copy.77
  61.4 0.2 fusion.28
  61.7 0.1 multiply_convert_fusion.1
  61.8 0.1 copy.31
  61.9 14.0 %all_gather.3 = bf16[16,2,128]{0,1,2:T(2,128)(2,1)S(1)} all-gather(bf16[16,2,16]{0,1,2:T(2,128)(2,1)S(1)} %copy.31), channel_id=1, replica_groups=mesh['groups'=2,'date'=4,'pix'=2,'chan'=2] {'date','chan'}, dimensions={2}, use_global_device_ids=true | all-gather | bytes 9216 | tf_op jit(solution)/shard_map/all_gather | solution.py:54
  75.8 0.1 copy.32
  75.9 1.4 fusion.16
  77.3 0.3 convolution_bitcast_fusion.10
  77.6 0.3 convolution_bitcast_fusion.4
  77.9 0.3 convolution_bitcast_fusion.7
  78.2 0.2 copy-done.9
  78.4 0.3 convolution_bitcast_fusion.11
  78.6 0.3 convolution_bitcast_fusion.5
  78.9 0.3 convolution_bitcast_fusion.6
  79.2 0.3 convolution_bitcast_fusion.8
  79.4 0.3 convolution_bitcast_fusion.9
  79.7 0.1 copy-done.4
  79.8 0.3 convolution_bitcast_fusion.3
  80.1 0.7 pad_maximum_fusion.2
  80.8 0.3 convolution_bitcast_fusion.1
  81.0 10.8 %psum.15 = f32[16,32,16]{1,2,0:T(8,128)} all-reduce(f32[16,32,16]{1,2,0:T(8,128)S(1)} %convolution_bitcast_fusion.1), channel_id=1, replica_groups=mesh['groups'=2,'date'=4,'pix'=2,'chan'=2] {'pix'}, use_global_device_ids=true, to_apply=%region_2.3 | all-reduce | flops 8192 | bytes 65536 | tf_op jit(solution)/shard_map/psum | solution.py:74
  91.8 57.2 %all-reduce.3.cloned.1.call-done = f32[3,3,64,32]{2,3,1,0:T(8,128)} async-done(((f32[3,3,64,32]{2,3,1,0:T(8,128)}), f32[3,3,64,32]{2,3,1,0:T(8,128)}) %all-reduce.3.cloned.1.call-update) | async-done | bytes 73744 | tf_op jit(solution)/shard_map/psum | solution.py:75
  149.0 1.6 %copy.115 = f32[3,3,64,32]{2,3,1,0:T(8,128)} copy(f32[3,3,64,32]{2,3,1,0:T(8,128)} %all-reduce.3.cloned.1.call-done) | data formatting | bytes 147456
  (34 shorter events, 0.2 us)
Async XLA Ops:
  7.2 20.3 %copy-start = (bf16[16,32,16]{1,2,0:T(8,128)(2,1)S(1)}, bf16[16,32,16]{1,2,0:T(8,128)(2,1)}, u32[]{:S(2)}) copy-start(bf16[16,32,16]{1,2,0:T(8,128)(2,1)} %param.10) | copy-start | bytes 49156
  7.2 15.9 %copy-start.1 = (bf16[16,2,64,128]{3,2,1,0:T(8,128)(2,1)S(1)}, bf16[16,2,64,128]{3,2,1,0:T(8,128)(2,1)}, u32[]{:S(2)}) copy-start(bf16[16,2,64,128]{3,2,1,0:T(8,128)(2,1)} %param.7) | copy-start | bytes 1572868
  7.2 53.4 %reduce-scatter.4.cloned.1.call-start = ((), (), s32[]{:S(2)}) async-start(), calls=%async_computation.2 | async-start | bytes 73728
  8.4 10.4 %collective-permute-start = (bf16[16,1,64,128]{3,2,1,0:T(8,128)(2,1)S(1)}, bf16[16,1,64,128]{3,2,1,0:T(8,128)(2,1)S(1)}, u32[]{:S(2)}, u32[]{:S(2)}) collective-permute-start(bf16[16,1,64,128]{3,2,1,0:T(8,128)(2,1)S(1)} %get-tuple-element.11), channel_id=1, source_target_pairs={{0,2},{1,3},{4,6},{5,7},{8,10},{9,11},{12,14},{13,15},{16,18},{17,... | collective-permute-start | bytes 786440 | tf_op jit(solution)/shard_map/ppermute | solution.py:12
  13.2 10.9 %copy-start.10 = (bf16[3,3,64,32]{2,3,1,0:T(8,128)(2,1)S(1)}, bf16[3,3,64,32]{2,3,1,0:T(8,128)(2,1)}, u32[]{:S(2)}) copy-start(bf16[3,3,64,32]{2,3,1,0:T(8,128)(2,1)} %param.8) | copy-start | bytes 110596
  13.3 9.8 %collective-permute-start.1 = (bf16[16,1,64,128]{3,2,1,0:T(8,128)(2,1)S(1)}, bf16[16,1,64,128]{3,2,1,0:T(8,128)(2,1)S(1)}, u32[]{:S(2)}, u32[]{:S(2)}) collective-permute-start(bf16[16,1,64,128]{3,2,1,0:T(8,128)(2,1)S(1)} %get-tuple-element.12), channel_id=1, source_target_pairs={{2,0},{3,1},{6,4},{7,5},{10,8},{11,9},{14,12},{15,13},{18,16},{19,... | collective-permute-start | bytes 786440 | tf_op jit(solution)/shard_map/ppermute | solution.py:15
  25.3 0.7 copy-start.15
  25.4 0.8 copy-start.2
  30.1 31.4 %copy-start.13 = (f32[16]{0:T(128)S(1)}, f32[16]{0:T(128)}, u32[]{:S(2)}) copy-start(f32[16]{0:T(128)} %param.11) | copy-start | bytes 196
  30.1 31.4 %copy-start.14 = (f32[16]{0:T(128)S(1)}, f32[16]{0:T(128)}, u32[]{:S(2)}) copy-start(f32[16]{0:T(128)} %param.12) | copy-start | bytes 196
  30.1 31.5 %copy-start.11 = (s32[2,16]{1,0:T(2,128)S(1)}, s32[2,16]{1,0:T(2,128)}, u32[]{:S(2)}) copy-start(s32[2,16]{1,0:T(2,128)} %param.13) | copy-start | bytes 388
  30.1 118.9 %all-reduce.3.cloned.1.call-start = ((), (), s32[]{:S(2)}) async-start(), calls=%async_computation.1 | async-start | bytes 294912 | tf_op jit(solution)/shard_map/psum | solution.py:75
  32.4 44.9 %copy-start.3 = (bf16[16,2,64,128]{3,2,1,0:T(8,128)(2,1)S(1)}, bf16[16,2,64,128]{3,2,1,0:T(8,128)(2,1)}, u32[]{:S(2)}) copy-start(bf16[16,2,64,128]{3,2,1,0:T(8,128)(2,1)} %copy-done.2) | copy-start | bytes 1572868
  61.6 16.2 %copy-start.12 = (f32[1,2,16]{2,0,1:T(1,128)}, f32[1,2,16]{2,0,1:T(1,128)S(1)}, u32[]{:S(2)}) copy-start(f32[1,2,16]{2,0,1:T(1,128)S(1)} %fusion.28) | copy-start | bytes 388
  77.3 1.0 copy-start.9
  77.3 1.3 copy-start.8
  77.6 1.3 copy-start.7
  77.9 1.3 copy-start.6
  78.1 1.3 copy-start.5
  78.6 1.2 copy-start.4
Sparse Core Ops, SparseCore 0:
  30.2 30.3 reduce-scatter.3
  80.9 68.0 all-reduce.2
where the time goes:
time: 158 us; the launch traced here: 157 us
  waiting for transfers between devices  92.5 us (59%)
  blocking collectives  24.7 us (16%)
  between operations  14.3 us (9%)
  local copies, waits for them, and re-layouts  8.89 us (6%)
  matrix products  8.7 us (6%)
  starting transfers between devices  6.36 us (4%)
  other arithmetic  1.98 us (1%)
    psum x1, waiting for transfers between devices, shards(): grad_spatial = lax.psum(spatial_part, ('date', 'pix'))  57.2 us
    unnamed x3, waiting for transfers between devices  28.2 us
    all_gather x1, blocking collectives, shards(): lax.all_gather(feature_grad, ('date', 'chan'), axis=2, tiled=True)  14 us
    psum x1, blocking collectives, shards(): grad_temporal = lax.psum(temporal_part, 'pix')  10.8 us
    unnamed x37, local copies, waits for them, and re-layouts  5.36 us
    ppermute x1, starting transfers between devices, with_halo(): lax.ppermute(lax.slice_in_dim(block, block.shape[dim] - width, None, axis...  4.86 us
    ppermute x1, waiting for transfers between devices, with_halo(): lax.ppermute(lax.slice_in_dim(block, 0, width, axis=dim), axis, backward)  4.27 us
    dot_general x9, matrix products, shards(): jnp.einsum('ticj,co->tioj', window, spatial_weight[row_off, col_off], pre...  4.27 us
  transfers between devices with their start and end apart: 4, of which 4 were waited for; matrix products, arithmetic and copies ran while one was open for 2% of the time, Pallas kernels for 0%

commit v1 on v0

--- a/solution.py
+++ b/solution.py
@@ -72,7 +72,7 @@
         rows_out.append(jnp.stack(cols_out))
     spatial_part = jnp.stack(rows_out)
     grad_temporal = lax.psum(temporal_part, "pix")
-    grad_spatial = lax.psum(spatial_part, ("date", "pix"))
+    grad_spatial = lax.psum(lax.psum(spatial_part, "pix"), "date")
     return (logits, grad_spatial, grad_temporal)
 
 

time: 158 us -> 146 us (0.924)
  waiting for transfers between devices: 92.5 us -> 82.9 us
  blocking collectives: 24.7 us -> 22.9 us
    psum x1 -> x2, waiting for transfers between devices: 57.2 us -> 47.5 us  [shards(): grad_spatial = lax.psum(lax.psum(spatial_part, 'pix'), 'date')]
    psum x1, blocking collectives: 10.8 us -> 8.96 us  [shards(): grad_temporal = lax.psum(temporal_part, 'pix')]
    unnamed x3 -> x4, waiting for transfers between devices: 28.2 us -> 28.2 us
  transfers between devices with their start and end apart: 4 -> 5, of which waited for: 4 -> 5; matrix products, arithmetic and copies ran while one was open for 2% -> 3% of each run, Pallas kernels for 0% -> 0%
where the time goes in v1:
time: 146 us
  waiting for transfers between devices  82.9 us (57%)
  blocking collectives  22.9 us (16%)
  between operations  14 us (10%)
  local copies, waits for them, and re-layouts  8.9 us (6%)
  matrix products  8.68 us (6%)
  starting transfers between devices  6.4 us (4%)
  other arithmetic  1.98 us (1%)
    psum x2, waiting for transfers between devices, shards(): grad_spatial = lax.psum(lax.psum(spatial_part, 'pix'), 'date')  47.5 us
    unnamed x4, waiting for transfers between devices  28.2 us
    all_gather x1, blocking collectives, shards(): lax.all_gather(feature_grad, ('date', 'chan'), axis=2, tiled=True)  14 us
    psum x1, blocking collectives, shards(): grad_temporal = lax.psum(temporal_part, 'pix')  8.96 us
    unnamed x37, local copies, waits for them, and re-layouts  5.37 us
    ppermute x1, starting transfers between devices, with_halo(): lax.ppermute(lax.slice_in_dim(block, block.shape[dim] - width, None, axis...  4.86 us
    ppermute x1, waiting for transfers between devices, with_halo(): lax.ppermute(lax.slice_in_dim(block, 0, width, axis=dim), axis, backward)  4.27 us
    dot_general x9, matrix products, shards(): jnp.einsum('ticj,co->tioj', window, spatial_weight[row_off, col_off], pre...  4.26 us
  transfers between devices with their start and end apart: 5, of which 5 were waited for; matrix products, arithmetic and copies ran while one was open for 3% of the time, Pallas kernels for 0%

profile of v1, /device:TPU:0, one launch (start us, length us, event | category | flops | bytes accessed | tf_op | source)
XLA Modules:
  0.0 145.7 jit_solution(8988503475884504636)
XLA Ops:
  7.2 1.1 fusion.79
  8.4 4.9 %collective-permute-start = (bf16[16,1,64,128]{3,2,1,0:T(8,128)(2,1)S(1)}, bf16[16,1,64,128]{3,2,1,0:T(8,128)(2,1)S(1)}, u32[]{:S(2)}, u32[]{:S(2)}) collective-permute-start(bf16[16,1,64,128]{3,2,1,0:T(8,128)(2,1)S(1)} %get-tuple-element.11), channel_id=1, source_target_pairs={{0,2},{1,3},{4,6},{5,7},{8,10},{9,11},{12,14},{13,15},{16,18},{17,... | collective-permute-start | bytes 786440 | tf_op jit(solution)/shard_map/ppermute | solution.py:12
  13.3 1.4 collective-permute-start.1
  14.7 1.3 fusion.47
  16.0 2.8 %collective-permute-done = bf16[16,1,64,128]{3,2,1,0:T(8,128)(2,1)S(1)} collective-permute-done((bf16[16,1,64,128]{3,2,1,0:T(8,128)(2,1)S(1)}, bf16[16,1,64,128]{3,2,1,0:T(8,128)(2,1)S(1)}, u32[]{:S(2)}, u32[]{:S(2)}) %collective-permute-start) | collective-permute-done | bytes 262176 | tf_op jit(solution)/shard_map/ppermute | solution.py:12
  18.8 4.3 %collective-permute-done.1 = bf16[16,1,64,128]{3,2,1,0:T(8,128)(2,1)S(1)} collective-permute-done((bf16[16,1,64,128]{3,2,1,0:T(8,128)(2,1)S(1)}, bf16[16,1,64,128]{3,2,1,0:T(8,128)(2,1)S(1)}, u32[]{:S(2)}, u32[]{:S(2)}) %collective-permute-start.1) | collective-permute-done | bytes 262176 | tf_op jit(solution)/shard_map/ppermute | solution.py:15
  23.0 1.1 fusion.5
  24.2 0.4 fusion.40
  24.5 0.4 fusion.51
  24.9 0.2 fusion.49
  25.1 0.2 fusion.44
  25.3 0.1 pad_maximum_fusion.1
  25.4 0.2 fusion.53
  25.6 0.2 fusion.42
  25.8 0.1 copy-done.15
  26.0 0.2 fusion.15
  26.2 1.2 multiply_convert_fusion
  27.4 0.2 convolution_bitcast_fusion.2
  27.6 0.8 copy.76
  28.4 1.7 %reshape.35 = f32[128,32]{1,0:T(8,128)} reshape(f32[128,2,16]{2,1,0:T(2,128)} %bitcast.179) | data formatting | bytes 32768
  30.1 2.2 %fusion.78 = (bf16[16,2,64,128]{3,2,1,0:T(8,128)(2,1)}, bf16[16,2,64,128]{3,2,1,0:T(8,128)(2,1)}, bf16[16,2,64,128]{3,2,1,0:T(8,128)(2,1)}, bf16[16,2,64,128]{3,...) fusion(bf16[16,4,64,130]{3,2,1,0:T(8,128)(2,1)S(1)} %fusion.5), kind=kLoop, calls=%fused_computation.104 | loop fusion | bytes 6291456 | tf_op jit(solution)/shard_map/slice | solution.py:29
  32.4 28.2 %reduce-scatter.4.cloned.1.call-done = f32[16,32]{1,0:T(8,128)} async-done(((f32[128,32]{1,0:T(8,128)}), f32[16,32]{1,0:T(8,128)}) %reduce-scatter.4.cloned.1.call-update) | async-done | bytes 2064
  60.6 0.8 reshape.36
  61.3 0.1 copy.77
  61.4 0.2 fusion.28
  61.7 0.1 multiply_convert_fusion.1
  61.8 0.1 copy.31
  61.8 14.0 %all_gather.3 = bf16[16,2,128]{0,1,2:T(2,128)(2,1)S(1)} all-gather(bf16[16,2,16]{0,1,2:T(2,128)(2,1)S(1)} %copy.31), channel_id=1, replica_groups=mesh['groups'=2,'date'=4,'pix'=2,'chan'=2] {'date','chan'}, dimensions={2}, use_global_device_ids=true | all-gather | bytes 9216 | tf_op jit(solution)/shard_map/all_gather | solution.py:54
  75.8 0.1 copy.32
  75.9 1.4 fusion.16
  77.3 0.3 convolution_bitcast_fusion.10
  77.6 0.3 convolution_bitcast_fusion.4
  77.9 0.3 convolution_bitcast_fusion.7
  78.1 0.2 copy-done.9
  78.3 0.3 convolution_bitcast_fusion.11
  78.6 0.3 convolution_bitcast_fusion.5
  78.9 0.3 convolution_bitcast_fusion.6
  79.1 0.3 convolution_bitcast_fusion.8
  79.4 0.3 convolution_bitcast_fusion.9
  79.7 0.1 copy-done.4
  79.8 0.3 convolution_bitcast_fusion.3
  80.1 0.7 pad_maximum_fusion.2
  80.8 0.0 all-reduce.6.cloned.1.call-start
  80.8 20.0 %all-reduce.4.cloned.1.call-done = f32[3,3,64,32]{2,3,1,0:T(8,128)} async-done(((f32[3,3,64,32]{2,3,1,0:T(8,128)}), f32[3,3,64,32]{2,3,1,0:T(8,128)}) %all-reduce.4.cloned.1.call-update) | async-done | bytes 73744 | tf_op jit(solution)/shard_map/psum | solution.py:75
  100.8 0.3 convolution_bitcast_fusion.1
  101.1 9.0 %psum.23 = f32[16,32,16]{1,2,0:T(8,128)} all-reduce(f32[16,32,16]{1,2,0:T(8,128)S(1)} %convolution_bitcast_fusion.1), channel_id=1, replica_groups=mesh['groups'=2,'date'=4,'pix'=2,'chan'=2] {'pix'}, use_global_device_ids=true, to_apply=%region_3.4 | all-reduce | flops 8192 | bytes 65536 | tf_op jit(solution)/shard_map/psum | solution.py:74
  110.0 27.6 %all-reduce.6.cloned.1.call-done = f32[3,3,64,32]{2,3,1,0:T(8,128)} async-done(((f32[3,3,64,32]{2,3,1,0:T(8,128)}), f32[3,3,64,32]{2,3,1,0:T(8,128)}) %all-reduce.6.cloned.1.call-update) | async-done | bytes 73744 | tf_op jit(solution)/shard_map/psum | solution.py:75
  137.6 1.6 %copy.116 = f32[3,3,64,32]{2,3,1,0:T(8,128)} copy(f32[3,3,64,32]{2,3,1,0:T(8,128)} %all-reduce.6.cloned.1.call-done) | data formatting | bytes 147456
  (37 shorter events, 0.3 us)
Async XLA Ops:
  7.2 20.2 %copy-start = (bf16[16,32,16]{1,2,0:T(8,128)(2,1)S(1)}, bf16[16,32,16]{1,2,0:T(8,128)(2,1)}, u32[]{:S(2)}) copy-start(bf16[16,32,16]{1,2,0:T(8,128)(2,1)} %param.10) | copy-start | bytes 49156
  7.2 15.9 %copy-start.1 = (bf16[16,2,64,128]{3,2,1,0:T(8,128)(2,1)S(1)}, bf16[16,2,64,128]{3,2,1,0:T(8,128)(2,1)}, u32[]{:S(2)}) copy-start(bf16[16,2,64,128]{3,2,1,0:T(8,128)(2,1)} %param.7) | copy-start | bytes 1572868
  7.2 53.4 %reduce-scatter.4.cloned.1.call-start = ((), (), s32[]{:S(2)}) async-start(), calls=%async_computation.3 | async-start | bytes 73728
  8.4 10.4 %collective-permute-start = (bf16[16,1,64,128]{3,2,1,0:T(8,128)(2,1)S(1)}, bf16[16,1,64,128]{3,2,1,0:T(8,128)(2,1)S(1)}, u32[]{:S(2)}, u32[]{:S(2)}) collective-permute-start(bf16[16,1,64,128]{3,2,1,0:T(8,128)(2,1)S(1)} %get-tuple-element.11), channel_id=1, source_target_pairs={{0,2},{1,3},{4,6},{5,7},{8,10},{9,11},{12,14},{13,15},{16,18},{17,... | collective-permute-start | bytes 786440 | tf_op jit(solution)/shard_map/ppermute | solution.py:12
  13.2 10.9 %copy-start.10 = (bf16[3,3,64,32]{2,3,1,0:T(8,128)(2,1)S(1)}, bf16[3,3,64,32]{2,3,1,0:T(8,128)(2,1)}, u32[]{:S(2)}) copy-start(bf16[3,3,64,32]{2,3,1,0:T(8,128)(2,1)} %param.8) | copy-start | bytes 110596
  13.3 9.8 %collective-permute-start.1 = (bf16[16,1,64,128]{3,2,1,0:T(8,128)(2,1)S(1)}, bf16[16,1,64,128]{3,2,1,0:T(8,128)(2,1)S(1)}, u32[]{:S(2)}, u32[]{:S(2)}) collective-permute-start(bf16[16,1,64,128]{3,2,1,0:T(8,128)(2,1)S(1)} %get-tuple-element.12), channel_id=1, source_target_pairs={{2,0},{3,1},{6,4},{7,5},{10,8},{11,9},{14,12},{15,13},{18,16},{19,... | collective-permute-start | bytes 786440 | tf_op jit(solution)/shard_map/ppermute | solution.py:15
  25.3 0.7 copy-start.15
  25.4 0.8 copy-start.2
  30.1 31.4 %copy-start.13 = (f32[16]{0:T(128)S(1)}, f32[16]{0:T(128)}, u32[]{:S(2)}) copy-start(f32[16]{0:T(128)} %param.11) | copy-start | bytes 196
  30.1 31.4 %copy-start.14 = (f32[16]{0:T(128)S(1)}, f32[16]{0:T(128)}, u32[]{:S(2)}) copy-start(f32[16]{0:T(128)} %param.12) | copy-start | bytes 196
  30.1 31.5 %copy-start.11 = (s32[2,16]{1,0:T(2,128)S(1)}, s32[2,16]{1,0:T(2,128)}, u32[]{:S(2)}) copy-start(s32[2,16]{1,0:T(2,128)} %param.13) | copy-start | bytes 388
  30.1 70.7 %all-reduce.4.cloned.1.call-start = ((), (), s32[]{:S(2)}) async-start(), calls=%async_computation.1 | async-start | bytes 294912 | tf_op jit(solution)/shard_map/psum | solution.py:75
  32.4 44.9 %copy-start.3 = (bf16[16,2,64,128]{3,2,1,0:T(8,128)(2,1)S(1)}, bf16[16,2,64,128]{3,2,1,0:T(8,128)(2,1)}, u32[]{:S(2)}) copy-start(bf16[16,2,64,128]{3,2,1,0:T(8,128)(2,1)} %copy-done.2) | copy-start | bytes 1572868
  61.6 16.2 %copy-start.12 = (f32[1,2,16]{2,0,1:T(1,128)}, f32[1,2,16]{2,0,1:T(1,128)S(1)}, u32[]{:S(2)}) copy-start(f32[1,2,16]{2,0,1:T(1,128)S(1)} %fusion.28) | copy-start | bytes 388
  77.3 1.0 copy-start.9
  77.3 1.3 copy-start.8
  77.6 1.3 copy-start.7
  77.9 1.3 copy-start.6
  78.1 1.3 copy-start.5
  78.6 1.2 copy-start.4
  80.8 56.9 %all-reduce.6.cloned.1.call-start = ((), (), s32[]{:S(2)}) async-start(), calls=%async_computation.2 | async-start | bytes 294912 | tf_op jit(solution)/shard_map/psum | solution.py:75
Sparse Core Ops, SparseCore 0:
  30.2 30.3 reduce-scatter.3
  80.9 19.8 all-reduce.3
  103.2 34.3 all-reduce.5
